TPU v7x, 256 devices: a whole 4x4x8 slice. The times are simulated.
256 devices in a mesh: grp: 2 (over core), gx: 16 (over x_lo, z), gy: 8 (over y, x_hi).
Axes of the slice: x: 4 (x_hi: 2, x_lo: 2; x = x_hi * 2 + x_lo), y: 4, z: 8, core: 2. Of those that a mesh axis runs over, the one named last changes fastest.
Arguments:
- velocity: float32 [3, 128, 128, 128], P(None, 'gx', ('grp', 'gy')), may hold values from -6 to 6
- moments: float32 [64, 128, 128, 128], P(None, 'gx', ('grp', 'gy')), may hold values from 0.1 to 1
- field: float32 [3, 128, 128, 128], P(None, 'gx', ('grp', 'gy')), may hold values from -6 to 6
- material: int32 [128, 128, 128], P('gx', ('grp', 'gy')), may hold values 0 or 1
- nozzle: int32 [256], replicated, may hold values from 0 to 2097025, as said below
- jet: float32 [3], replicated, may hold values from -2 to 2
- inlet: float32 [64], replicated, may hold values from 0.2 to 1
- rates: float32 [64, 32], replicated, may hold values from 0.02 to 0.8
- partners: int32 [64, 32], replicated, may hold values from 0 to 63
Outputs:
- new_velocity: float32 [3, 128, 128, 128], P(None, 'gx', ('grp', 'gy'))
- new_moments: float32 [64, 128, 128, 128], P(None, 'gx', ('grp', 'gy'))
Inputs may be any that keep to these rules, and one draw needn't show every extreme that they name: `nozzle`: distinct cells of the two layers at z = 0 and 1: each entry is (x * 128 + y) * 128 + z with z 0 or 1.
All inputs are finite; a program needn't handle non-finite values. No bound on the sum of `material` on one device may be relied on, other than what follows from the above.
Results may differ from a plain program's by a relative error of at most 0.0032.
Values sent between devices are 32-bit elements; how exact they have to be, the bound alone decides.
A program may use at most 128 MiB of HBM per device.

v0:
```python
import functools
import math

import jax
import jax.numpy as jnp
import numpy as np
from jax import lax
from jax.experimental import pallas as pl
from jax.experimental.pallas import tpu as pltpu
from jax.sharding import PartitionSpec as P

step_size = 0.2
viscosity = 0.5
screening = 0.0001
MESH = pl.DeviceIdType.MESH
SIDE = 8
PITCH = 10
SLOTS = 16
LANES = 128


def wave_of(length):
    index = np.arange(2 * length)
    return np.where(index <= length, index, index - length)


def real_basis(length):
    span = 2 * length
    index = np.arange(span)
    angle = 2.0 * math.pi / span * ((wave_of(length)[:, None] * np.arange(length)[None, :]) % span)
    return np.where(index[:, None] <= length, np.cos(angle), np.sin(angle))


def real_weights(length):
    span = 2 * length
    weights = np.full(span, 2.0 / span)
    weights[0] = weights[length] = 1.0 / span
    return weights


def wave_factors(length):
    return 2.0 - 2.0 * np.cos(2.0 * math.pi * wave_of(length) / (2 * length))


def tables(full_x, full_y, depth):
    bricks_x, bricks_y = full_x // SIDE, full_y // SIDE
    basis_x, basis_y, basis_z = real_basis(full_x), real_basis(full_y), real_basis(depth)
    inverse_x = basis_x * real_weights(full_x)[:, None]
    inverse_y = basis_y * real_weights(full_y)[:, None]
    inverse_z = basis_z * real_weights(depth)[:, None]
    forward_x = np.zeros((2 * full_x, bricks_x * SLOTS))
    backward_x = np.zeros((bricks_x * SLOTS, 2 * full_x))
    for brick in range(bricks_x):
        for slot in range(PITCH):
            x = SIDE * brick + (slot if slot < SIDE else (-1 if slot == SIDE else SIDE))
            if 0 <= x < full_x:
                forward_x[:, brick * SLOTS + slot] = basis_x[:, x]
                backward_x[brick * SLOTS + slot] = inverse_x[:, x]
    masks = np.zeros((bricks_y, SLOTS, LANES))
    for brick in range(bricks_y):
        for slot in range(PITCH):
            for lane in range(LANES):
                source = (lane - (SIDE * brick - 1)) % LANES
                if slot < SIDE:
                    y = SIDE * brick - 1 + source - PITCH * slot
                    inside = 0 <= source - PITCH * slot < PITCH
                else:
                    offset = source - PITCH * SIDE - SIDE * (slot - SIDE)
                    y = SIDE * brick + offset
                    inside = 0 <= offset < SIDE
                if inside and 0 <= y < full_y:
                    masks[brick, slot, lane] = 1.0
    f32 = lambda array: jnp.asarray(np.asarray(array, np.float32))
    return dict(
        basis_z=f32(basis_z),
        inverse_z=f32(inverse_z),
        forward_x=f32(forward_x),
        backward_x=f32(backward_x),
        forward_y=f32(basis_y.T),
        backward_y=f32(inverse_y),
        factor_x=f32(wave_factors(full_x)[:, None]),
        factor_y=f32(wave_factors(full_y)[None, :]),
        factor_z=f32(wave_factors(depth) + screening),
        masks=f32(masks.reshape(bricks_y * SLOTS, LANES)),
    )


def turn_of(slot):
    return (-PITCH * slot if slot < SIDE else 1 - PITCH * SIDE - SIDE * (slot - SIDE)) % LANES


def roll(values, shift, axis):
    shift = shift % values.shape[axis]
    return values if shift == 0 else pltpu.roll(values, shift, axis)


def dot(first, second, dims=((1,), (0,))):
    return lax.dot_general(
        first,
        second,
        (dims, ((), ())),
        precision=lax.Precision.HIGHEST,
        preferred_element_type=jnp.float32,
    )


def kernel(
    velocity, field, material, moments, nozzle, jet, inlet, rates, partners,
    basis_z, inverse_z, forward_x, backward_x, forward_y, backward_y,
    factor_x, factor_y, factor_z, masks,
    new_velocity, new_moments,
    ext, grown, result, face_x, face_y, cut_y, coef,
    source, send_a, recv_a, send_b, recv_b, send_c, recv_c, send_d, recv_d, poten,
    load_sem, store_sem, halo_send, halo_recv, ssem, rsem,
):
    wide = 16
    classes = rates.shape[0]
    rows = SIDE * SIDE
    me_x = lax.axis_index("gx")
    me_grp, me_gy = lax.axis_index("grp"), lax.axis_index("gy")
    groups = lax.axis_size("gy")
    me_y = me_grp * groups + me_gy

    def along_x(index):
        return {"gx": index}

    def along_y(index):
        return {"grp": index // groups, "gy": lax.rem(index, groups)}

    load = pltpu.make_async_copy(moments, ext.at[pl.ds(0, classes)], load_sem)
    load.start()
    barrier = pltpu.get_barrier_semaphore()

    @pl.loop(1, wide)
    def _(step):
        pl.semaphore_signal(
            barrier, inc=1, device_id=along_x(lax.rem(me_x + step, wide)), device_id_type=MESH
        )
        pl.semaphore_signal(
            barrier, inc=1, device_id=along_y(lax.rem(me_y + step, wide)), device_id_type=MESH
        )

    lane = lax.broadcasted_iota(jnp.int32, (SIDE, LANES), 1)
    row = lax.broadcasted_iota(jnp.int32, (SIDE, LANES), 0)
    not_first, not_last = lane != 0, lane != LANES - 1

    def up_z(v):
        return jnp.where(not_last, roll(v, -1, 1), 0.0)

    def down_z(v):
        return jnp.where(not_first, roll(v, 1, 1), 0.0)

    def current_at(x):
        m = [ext[classes + a, SIDE * x : SIDE * x + SIDE] for a in range(3)]
        f = [field[a, x] for a in range(3)]
        return (
            m[1] * f[2] - m[2] * f[1],
            m[2] * f[0] - m[0] * f[2],
            m[0] * f[1] - m[1] * f[0],
        )

    for x in range(SIDE):
        liquid = material[x].astype(jnp.float32)
        for a in range(3):
            ext[classes + a, SIDE * x : SIDE * x + SIDE] = velocity[a, x] * liquid
    currents = [current_at(x) for x in range(SIDE)]
    for x in range(SIDE):
        c1, c2 = currents[x][1], currents[x][2]
        s = jnp.where(row < SIDE - 1, roll(c1, -1, 0), 0.0) - jnp.where(row > 0, roll(c1, 1, 0), 0.0)
        s = s + up_z(c2) - down_z(c2)
        if x + 1 < SIDE:
            s = s + currents[x + 1][0]
        if x > 0:
            s = s - currents[x - 1][0]
        source[PITCH * x + 1 : PITCH * x + 1 + SIDE] = 0.5 * s
        source[PITCH * x : PITCH * x + 1] = 0.5 * c1[0:1]
        source[PITCH * x + PITCH - 1 : PITCH * x + PITCH] = -0.5 * c1[SIDE - 1 : SIDE]
    edge = PITCH * SIDE
    source[edge : edge + SIDE] = 0.5 * currents[0][0]
    source[edge + SIDE : edge + 2 * SIDE] = -0.5 * currents[SIDE - 1][0]
    source[edge + 2 * SIDE :] = jnp.zeros((LANES - edge - 2 * SIDE, LANES), jnp.float32)
    send_a[...] = dot(basis_z[...], source[...], ((1,), (1,)))

    pl.semaphore_wait(barrier, 2 * (wide - 1))

    def exchange(phase, send, recv, me, target):
        mine = pl.ds(pl.multiple_of(me * wide, wide), wide)

        def start(step):
            other = lax.rem(me + step, wide)
            pltpu.make_async_remote_copy(
                src_ref=send.at[pl.ds(pl.multiple_of(other * wide, wide), wide)],
                dst_ref=recv.at[mine],
                send_sem=ssem.at[phase],
                recv_sem=rsem.at[phase],
                device_id=target(other),
                device_id_type=MESH,
            ).start()

        pl.loop(1, wide)(start)
        recv[mine] = send[mine]

    def arrived(phase, send, recv):
        part = pl.ds(0, (wide - 1) * wide)
        pltpu.make_async_copy(recv.at[part], recv.at[part], rsem.at[phase]).wait()

    def sent(phase, send):
        part = pl.ds(0, (wide - 1) * wide)
        pltpu.make_async_copy(send.at[part], send.at[part], ssem.at[phase]).wait()

    exchange(0, send_a, recv_a, me_y, along_y)

    load.wait()
    flat = ext.reshape((classes + 3) * rows, LANES)
    for side in range(2):
        cut_y[side] = flat[pl.ds(side * (SIDE - 1), (classes + 3) * SIDE, stride=SIDE), :].reshape(
            classes + 3, SIDE, LANES
        )
    lower_x, upper_x = lax.rem(me_x + wide - 1, wide), lax.rem(me_x + 1, wide)
    lower_y, upper_y = lax.rem(me_y + wide - 1, wide), lax.rem(me_y + 1, wide)
    halos = []
    for number, (src, dst, device) in enumerate(
        [
            (cut_y.at[0], face_y.at[1], along_y(lower_y)),
            (cut_y.at[1], face_y.at[0], along_y(upper_y)),
            (ext.at[:, pl.ds(0, SIDE)], face_x.at[1], along_x(lower_x)),
            (ext.at[:, pl.ds(rows - SIDE, SIDE)], face_x.at[0], along_x(upper_x)),
        ]
    ):
        copy = pltpu.make_async_remote_copy(
            src_ref=src,
            dst_ref=dst,
            send_sem=halo_send.at[number],
            recv_sem=halo_recv.at[number],
            device_id=device,
            device_id_type=MESH,
        )
        copy.start()
        halos.append(copy)

    square = lax.broadcasted_iota(jnp.int32, (classes, LANES), 1)
    owner = lax.broadcasted_iota(jnp.int32, (classes, LANES), 0)
    full = jnp.zeros((classes, LANES), jnp.float32)
    for r in range(rates.shape[1]):
        full = full + jnp.where(partners[:, r : r + 1] == square, rates[:, r : r + 1], 0.0)
    turned = jnp.concatenate([full, jnp.zeros((LANES - classes, LANES), jnp.float32)], 0).T[:classes]
    low = jnp.where(square < owner, full + turned, jnp.where(square == owner, full, 0.0))
    full = full - jnp.where(owner == classes - 1, low, 0.0)
    low = jnp.where(owner > 0, roll(low, 1, 0), 0.0)
    both = jnp.concatenate([low, full], 0)
    high_part = both.astype(jnp.bfloat16).astype(jnp.float32)
    low_part = both - high_part
    column = lax.broadcasted_iota(jnp.int32, (2 * classes, LANES), 1)
    weights = jnp.where(column < classes, high_part, roll(low_part, classes, 1)).astype(jnp.bfloat16)
    flat_grown = grown.reshape(classes * rows, LANES)

    def grow(pair):
        parts = [
            flat[pl.ds(2 * pair + h, classes, stride=rows), :].astype(jnp.bfloat16) for h in range(2)
        ]
        narrow = jnp.concatenate(parts, 1)
        mixed = jnp.dot(
            weights, jnp.concatenate([narrow, narrow], 0), preferred_element_type=jnp.float32
        )
        for h in range(2):
            n = parts[h].astype(jnp.float32)
            piece = mixed[:, h * LANES : (h + 1) * LANES]
            flat_grown[pl.ds(2 * pair + h, classes, stride=rows), :] = (
                roll(n, 1, 0) * piece[:classes] - n * piece[classes:]
            )

    pl.loop(0, rows // 2)(grow)

    cell = lax.broadcasted_iota(jnp.int32, (rows, 1), 0)
    full_y = SIDE * wide
    base = ((me_x * SIDE + cell // SIDE) * full_y + me_y * SIDE + cell % SIDE) * LANES
    hit = [
        jnp.max(jnp.where(nozzle[...] == base + z, 1.0, 0.0), axis=1, keepdims=True) for z in range(2)
    ]
    deep = lax.broadcasted_iota(jnp.int32, (rows, LANES), 1)
    coef[8] = jnp.where(deep == 0, hit[0], jnp.where(deep == 1, hit[1], 0.0))

    arrived(0, send_a, recv_a)
    strips = [jnp.zeros((wide, LANES), jnp.float32) for _ in range(PITCH)]
    for by in range(wide):
        line = roll(recv_a[by * wide : (by + 1) * wide], SIDE * by - 1, 1)
        for slot in range(PITCH):
            strips[slot] = strips[slot] + line * masks[by * SLOTS + slot : by * SLOTS + slot + 1]
    for slot in range(SLOTS):
        send_b[pl.ds(slot, wide, stride=SLOTS), :] = (
            roll(strips[slot], turn_of(slot), 1)
            if slot < PITCH
            else jnp.zeros((wide, LANES), jnp.float32)
        )
    exchange(1, send_b, recv_b, me_x, along_x)

    wave = factor_z[me_y * wide + me_x]
    inverse = -1.0 / ((factor_x[...] + wave) + factor_y[...])
    arrived(1, send_b, recv_b)
    plane = dot(dot(forward_x[...], recv_b[...]), forward_y[...]) * inverse
    send_c[...] = dot(backward_x[...], dot(plane, backward_y[...]))
    exchange(2, send_c, recv_c, me_x, along_x)
    arrived(2, send_c, recv_c)
    strips = [
        roll(recv_c[pl.ds(slot, wide, stride=SLOTS), :], -turn_of(slot), 1) for slot in range(PITCH)
    ]
    for by in range(wide):
        total = jnp.zeros((wide, LANES), jnp.float32)
        for slot in range(PITCH):
            total = total + strips[slot] * masks[by * SLOTS + slot : by * SLOTS + slot + 1]
        send_d[by * wide : (by + 1) * wide] = roll(total, 1 - SIDE * by, 1)
    exchange(3, send_d, recv_d, me_y, along_y)

    for copy in halos:
        copy.wait_recv()
    has_x = [(me_x > 0).astype(jnp.float32), (me_x < wide - 1).astype(jnp.float32)]
    has_y = [(me_y > 0).astype(jnp.float32), (me_y < wide - 1).astype(jnp.float32)]

    def moving_at(a, x):
        if x < 0:
            return face_x[0, classes + a] * has_x[0]
        if x >= SIDE:
            return face_x[1, classes + a] * has_x[1]
        return ext[classes + a, SIDE * x : SIDE * x + SIDE]

    def around_y(a, x):
        here = moving_at(a, x)
        below = jnp.where(row == 0, face_y[0, classes + a, x : x + 1] * has_y[0], roll(here, 1, 0))
        above = jnp.where(
            row == SIDE - 1, face_y[1, classes + a, x : x + 1] * has_y[1], roll(here, -1, 0)
        )
        return below, above

    for x in range(SIDE):
        part = slice(SIDE * x, SIDE * x + SIDE)
        stop = coef[8, part]
        scale = step_size * material[x].astype(jnp.float32) * (1.0 - stop)
        total = jnp.zeros((SIDE, LANES), jnp.float32)
        for a in range(3):
            here = moving_at(a, x)
            if a == 0:
                below, above = moving_at(0, x - 1), moving_at(0, x + 1)
            elif a == 1:
                below, above = around_y(1, x)
            else:
                below, above = down_z(here), up_z(here)
            up, down = 0.5 * (here + above), 0.5 * (below + here)
            total = total + (jnp.maximum(up, 0.0) - jnp.minimum(down, 0.0))
            plus, minus = -scale * jnp.minimum(up, 0.0), scale * jnp.maximum(down, 0.0)
            if a == 0:
                if x == 0:
                    minus = minus * has_x[0]
                if x == SIDE - 1:
                    plus = plus * has_x[1]
            elif a == 1:
                minus = jnp.where(row == 0, minus * has_y[0], minus)
                plus = jnp.where(row == SIDE - 1, plus * has_y[1], plus)
            else:
                minus = jnp.where(not_first, minus, 0.0)
                plus = jnp.where(not_last, plus, 0.0)
            coef[2 * a + 1, part] = minus
            coef[2 * a + 2, part] = plus
        coef[0, part] = 1.0 - stop - scale * total
        coef[7, part] = scale

    def advance(k):
        fill = inlet[k]
        for x in range(SIDE):
            part = slice(SIDE * x, SIDE * x + SIDE)
            here = ext[k, part]
            below = face_x[0, k] if x == 0 else ext[k, SIDE * x - SIDE : SIDE * x]
            above = face_x[1, k] if x == SIDE - 1 else ext[k, SIDE * x + SIDE : SIDE * x + 2 * SIDE]
            left = jnp.where(row == 0, face_y[0, k, x : x + 1], roll(here, 1, 0))
            right = jnp.where(row == SIDE - 1, face_y[1, k, x : x + 1], roll(here, -1, 0))
            result[k, part] = (
                (coef[0, part] * here + coef[7, part] * grown[k, part])
                + (coef[1, part] * below + coef[2, part] * above)
                + (coef[3, part] * left + coef[4, part] * right)
                + (coef[5, part] * roll(here, 1, 1) + coef[6, part] * roll(here, -1, 1))
                + coef[8, part] * fill
            )

    pl.loop(0, classes)(advance)
    store = pltpu.make_async_copy(result, new_moments, store_sem)
    store.start()

    arrived(3, send_d, recv_d)
    poten[...] = dot(recv_d[...], inverse_z[...], ((0,), (0,)))
    for x in range(SIDE):
        part = slice(SIDE * x, SIDE * x + SIDE)

        def pot(x):
            if x < 0:
                return poten[edge : edge + SIDE]
            if x >= SIDE:
                return poten[edge + SIDE : edge + 2 * SIDE]
            return poten[PITCH * x + 1 : PITCH * x + 1 + SIDE]

        low_y = poten[PITCH * x : PITCH * x + SIDE]
        high_y = poten[PITCH * x + 2 : PITCH * x + 2 + SIDE]
        middle = pot(x)
        gradient = (
            0.5 * (pot(x + 1) - pot(x - 1)),
            0.5 * (high_y - low_y),
            0.5 * (up_z(middle) - down_z(middle)),
        )
        c = current_at(x)
        d = [c[a] - gradient[a] for a in range(3)]
        f = [field[a, x] for a in range(3)]
        lorentz = (d[1] * f[2] - d[2] * f[1], d[2] * f[0] - d[0] * f[2], d[0] * f[1] - d[1] * f[0])
        liquid = material[x].astype(jnp.float32)
        stop = coef[8, part] > 0.5
        for a in range(3):
            here = moving_at(a, x)
            below, above = around_y(a, x)
            spread = (
                (moving_at(a, x - 1) + moving_at(a, x + 1))
                + (below + above)
                + (down_z(here) + up_z(here))
                - 6.0 * here
            )
            value = liquid * (here + step_size * (lorentz[a] + viscosity * spread))
            new_velocity[a, x] = jnp.where(stop, jet[a], value)

    for phase, buffer in enumerate((send_a, send_b, send_c, send_d)):
        sent(phase, buffer)
    for copy in halos:
        copy.wait_send()
    store.wait()


def local(velocity, moments, field, material, nozzle, jet, inlet, rates, partners):
    width_x = lax.axis_size("gx")
    width_y = lax.axis_size("grp") * lax.axis_size("gy")
    cells_x, cells_y, depth = material.shape
    classes = moments.shape[0]
    rows = cells_x * cells_y
    table = tables(cells_x * width_x, cells_y * width_y, depth)
    vmem = pl.BlockSpec(memory_space=pltpu.VMEM)
    smem = pl.BlockSpec(memory_space=pltpu.SMEM)
    anywhere = pl.BlockSpec(memory_space=pl.ANY)
    f32 = jnp.float32
    square = pltpu.VMEM((2 * LANES, LANES), f32)
    new_velocity, new_moments = pl.pallas_call(
        kernel,
        out_shape=(
            jax.ShapeDtypeStruct(velocity.shape, f32),
            jax.ShapeDtypeStruct((classes, rows, depth), f32),
        ),
        in_specs=[vmem, vmem, vmem, anywhere, vmem, smem, smem, vmem, vmem]
        + [vmem] * 8 + [smem, vmem],
        out_specs=(vmem, anywhere),
        scratch_shapes=[
            pltpu.VMEM((classes + 3, rows, LANES), f32),
            pltpu.VMEM((classes, rows, LANES), f32),
            pltpu.VMEM((classes, rows, LANES), f32),
            pltpu.VMEM((2, classes + 3, SIDE, LANES), f32),
            pltpu.VMEM((2, classes + 3, SIDE, LANES), f32),
            pltpu.VMEM((2, classes + 3, SIDE, LANES), f32),
            pltpu.VMEM((9, rows, LANES), f32),
            pltpu.VMEM((LANES, LANES), f32),
            square, square, square, square, square, square, square, square,
            pltpu.VMEM((LANES, LANES), f32),
            pltpu.SemaphoreType.DMA,
            pltpu.SemaphoreType.DMA,
            pltpu.SemaphoreType.DMA((4,)),
            pltpu.SemaphoreType.DMA((4,)),
            pltpu.SemaphoreType.DMA((4,)),
            pltpu.SemaphoreType.DMA((4,)),
        ],
        compiler_params=pltpu.CompilerParams(
            collective_id=0, has_side_effects=True, vmem_limit_bytes=48 * 1024 * 1024
        ),
    )(
        velocity, field, material, moments.reshape(classes, rows, depth),
        nozzle.reshape(1, -1), jet, inlet, rates, partners,
        table["basis_z"], table["inverse_z"], table["forward_x"], table["backward_x"],
        table["forward_y"], table["backward_y"], table["factor_x"], table["factor_y"],
        table["factor_z"], table["masks"],
    )
    return (new_velocity, new_moments.reshape(moments.shape))


def solution(mesh):
    bricks = P(None, "gx", ("grp", "gy"), None)
    return jax.shard_map(
        local,
        mesh=mesh,
        in_specs=(bricks, bricks, bricks, P("gx", ("grp", "gy"), None), P(), P(), P(), P(), P()),
        out_specs=(bricks, bricks),
        check_vma=False,
    )
```

profile of v0, /device:TPU:1, one launch (start us, length us, event | category | flops | bytes accessed | tf_op | source)
XLA Modules:
  0.0 63.7 jit_solution(7308857676831010950)
XLA Ops:
  0.6 0.8 %copy.21.rates = f32[64,32]{1,0:T(8,128)S(1)} copy(f32[64,32]{0,1:T(8,128)} %param.26) | data formatting | bytes 16384 | tf_op args[7]
  1.4 0.8 %copy.22.partners = s32[64,32]{1,0:T(8,128)S(1)} copy(s32[64,32]{0,1:T(8,128)} %param.27) | data formatting | bytes 16384 | tf_op args[8]
  2.2 0.0 copy-start
  2.2 1.6 %copy-done = f32[64,8,8,128]{3,2,1,0:T(8,128)S(1)} copy-done((f32[64,8,8,128]{3,2,1,0:T(8,128)S(1)}, f32[64,8,8,128]{3,2,1,0:T(8,128)}, u32[]{:S(2)}) %copy-start) | copy-done | bytes 2097176
  3.8 0.0 copy-start.1
  3.8 0.9 %copy-done.1 = f32[256,128]{1,0:T(8,128)S(1)} copy-done((f32[256,128]{1,0:T(8,128)S(1)}, f32[256,128]{1,0:T(8,128)}, u32[]{:S(2)}) %copy-start.1) | copy-done | bytes 131096
  4.7 0.0 copy-start.2
  4.7 0.9 %copy-done.2 = f32[256,256]{1,0:T(8,128)S(1)} copy-done((f32[256,256]{1,0:T(8,128)S(1)}, f32[256,256]{1,0:T(8,128)}, u32[]{:S(2)}) %copy-start.2) | copy-done | bytes 262168
  5.7 0.9 %copy-done.3 = f32[256,256]{1,0:T(8,128)S(1)} copy-done((f32[256,256]{1,0:T(8,128)S(1)}, f32[256,256]{1,0:T(8,128)}, u32[]{:S(2)}) %copy-start.3) | copy-done | bytes 262168
  6.6 0.9 %copy-done.4 = f32[256,128]{1,0:T(8,128)S(1)} copy-done((f32[256,128]{1,0:T(8,128)S(1)}, f32[256,128]{1,0:T(8,128)}, u32[]{:S(2)}) %copy-start.4) | copy-done | bytes 131096
  7.5 0.9 %copy-done.5 = f32[256,1]{1,0:T(8,128)S(1)} copy-done((f32[256,1]{1,0:T(8,128)S(1)}, f32[256,1]{1,0:T(8,128)}, u32[]{:S(2)}) %copy-start.5) | copy-done | bytes 1048
  8.4 0.9 %copy-done.6 = f32[128,256]{1,0:T(8,128)S(1)} copy-done((f32[128,256]{1,0:T(8,128)S(1)}, f32[128,256]{1,0:T(8,128)}, u32[]{:S(2)}) %copy-start.6) | copy-done | bytes 131096
  9.3 0.9 %copy-done.7 = f32[256,128]{1,0:T(8,128)S(1)} copy-done((f32[256,128]{1,0:T(8,128)S(1)}, f32[256,128]{1,0:T(8,128)}, u32[]{:S(2)}) %copy-start.7) | copy-done | bytes 131096
  10.2 0.9 %copy-done.8 = f32[3,8,8,128]{3,2,1,0:T(8,128)S(1)} copy-done((f32[3,8,8,128]{3,2,1,0:T(8,128)S(1)}, f32[3,8,8,128]{3,2,1,0:T(8,128)}, u32[]{:S(2)}) %copy-start.8) | copy-done | bytes 98328
  11.1 0.9 %copy-done.9 = f32[3,8,8,128]{3,2,1,0:T(8,128)S(1)} copy-done((f32[3,8,8,128]{3,2,1,0:T(8,128)S(1)}, f32[3,8,8,128]{3,2,1,0:T(8,128)}, u32[]{:S(2)}) %copy-start.9) | copy-done | bytes 98328
  12.0 0.8 %copy-done.10 = s32[8,8,128]{2,1,0:T(8,128)S(1)} copy-done((s32[8,8,128]{2,1,0:T(8,128)S(1)}, s32[8,8,128]{2,1,0:T(8,128)}, u32[]{:S(2)}) %copy-start.10) | copy-done | bytes 32792
  12.8 0.7 %copy-done.11 = s32[256]{0:T(256)S(1)} copy-done((s32[256]{0:T(256)S(1)}, s32[256]{0:T(256)}, u32[]{:S(2)}) %copy-start.11) | copy-done | bytes 1048
  13.5 0.7 %copy-done.12 = f32[256]{0:T(256)S(1)} copy-done((f32[256]{0:T(256)S(1)}, f32[256]{0:T(256)}, u32[]{:S(2)}) %copy-start.12) | copy-done | bytes 1048
  14.2 0.7 %copy-done.13 = f32[1,256]{1,0:T(1,128)S(1)} copy-done((f32[1,256]{1,0:T(1,128)S(1)}, f32[1,256]{1,0:T(1,128)}, u32[]{:S(2)}) %copy-start.13) | copy-done | bytes 1048
  14.8 0.7 %copy-done.14 = f32[3]{0:T(128)S(1)} copy-done((f32[3]{0:T(128)S(1)}, f32[3]{0:T(128)}, u32[]{:S(2)}) %copy-start.14) | copy-done | bytes 36
  15.5 0.7 %copy-done.15 = f32[64]{0:T(128)S(1)} copy-done((f32[64]{0:T(128)S(1)}, f32[64]{0:T(128)}, u32[]{:S(2)}) %copy-start.15) | copy-done | bytes 280
  16.1 45.6 %shard_map.194 = (f32[3,8,8,128]{3,2,1,0:T(8,128)S(1)}, f32[64,64,128]{2,1,0:T(8,128)S(1)}) custom-call(f32[3,8,8,128]{3,2,1,0:T(8,128)S(1)} %copy-done.8, f32[3,8,8,128]{3,2,1,0:T(8,128)S(1)} %copy-done.9, s32[8,8,128]{2,1,0:T(8,128)S(1)} %copy-done.10, f32[64,64,128]{2,1,0:T(8,128)S(1)} %bitcast.3, s32[1,256]{1,0:T(1,128)S(1)} %bitcast.5, ...), custom_call_target="tpu_custom_call" | custom-call | tf_op jit(solution)/shard_map/pallas_call | solution.py:444
  61.8 0.6 %copy.25 = f32[3,8,8,128]{3,2,1,0:T(8,128)} copy(f32[3,8,8,128]{3,2,1,0:T(8,128)S(1)} %get-tuple-element.8) | data formatting | bytes 196608
  62.4 1.3 %copy.26 = f32[64,8,8,128]{3,2,1,0:T(8,128)} copy(f32[64,8,8,128]{3,2,1,0:T(8,128)S(1)} %bitcast.4) | data formatting | bytes 4194304
  (13 shorter events, 0.0 us)
Async XLA Ops:
  2.2 1.6 %copy-start = (f32[64,8,8,128]{3,2,1,0:T(8,128)S(1)}, f32[64,8,8,128]{3,2,1,0:T(8,128)}, u32[]{:S(2)}) copy-start(f32[64,8,8,128]{3,2,1,0:T(8,128)} %param.20) | copy-start | bytes 6291460
  3.8 0.9 %copy-start.1 = (f32[256,128]{1,0:T(8,128)S(1)}, f32[256,128]{1,0:T(8,128)}, u32[]{:S(2)}) copy-start(f32[256,128]{1,0:T(8,128)} %constant.19.clone.inverse_z.backward_y) | copy-start | bytes 393220
  4.7 0.9 %copy-start.2 = (f32[256,256]{1,0:T(8,128)S(1)}, f32[256,256]{1,0:T(8,128)}, u32[]{:S(2)}) copy-start(f32[256,256]{1,0:T(8,128)} %constant.21.clone.backward_x) | copy-start | bytes 786436
  5.7 0.9 %copy-start.3 = (f32[256,256]{1,0:T(8,128)S(1)}, f32[256,256]{1,0:T(8,128)}, u32[]{:S(2)}) copy-start(f32[256,256]{1,0:T(8,128)} %constant.20.clone.forward_x) | copy-start | bytes 786436
  6.6 0.9 %copy-start.4 = (f32[256,128]{1,0:T(8,128)S(1)}, f32[256,128]{1,0:T(8,128)}, u32[]{:S(2)}) copy-start(f32[256,128]{1,0:T(8,128)} %constant.26.clone.masks) | copy-start | bytes 393220
  7.5 0.9 %copy-start.5 = (f32[256,1]{1,0:T(8,128)S(1)}, f32[256,1]{1,0:T(8,128)}, u32[]{:S(2)}) copy-start(f32[256,1]{1,0:T(8,128)} %constant.23.clone.factor_x) | copy-start | bytes 3076
  8.4 0.9 %copy-start.6 = (f32[128,256]{1,0:T(8,128)S(1)}, f32[128,256]{1,0:T(8,128)}, u32[]{:S(2)}) copy-start(f32[128,256]{1,0:T(8,128)} %constant.22.clone.forward_y) | copy-start | bytes 393220
  9.3 0.9 %copy-start.7 = (f32[256,128]{1,0:T(8,128)S(1)}, f32[256,128]{1,0:T(8,128)}, u32[]{:S(2)}) copy-start(f32[256,128]{1,0:T(8,128)} %constant.18.clone.basis_z) | copy-start | bytes 393220
  10.2 0.9 %copy-start.8 = (f32[3,8,8,128]{3,2,1,0:T(8,128)S(1)}, f32[3,8,8,128]{3,2,1,0:T(8,128)}, u32[]{:S(2)}) copy-start(f32[3,8,8,128]{3,2,1,0:T(8,128)} %velocity.1) | copy-start | bytes 294916
  11.1 0.9 %copy-start.9 = (f32[3,8,8,128]{3,2,1,0:T(8,128)S(1)}, f32[3,8,8,128]{3,2,1,0:T(8,128)}, u32[]{:S(2)}) copy-start(f32[3,8,8,128]{3,2,1,0:T(8,128)} %field.1) | copy-start | bytes 294916
  12.0 0.8 %copy-start.10 = (s32[8,8,128]{2,1,0:T(8,128)S(1)}, s32[8,8,128]{2,1,0:T(8,128)}, u32[]{:S(2)}) copy-start(s32[8,8,128]{2,1,0:T(8,128)} %material.1) | copy-start | bytes 98308
  12.8 0.7 %copy-start.11 = (s32[256]{0:T(256)S(1)}, s32[256]{0:T(256)}, u32[]{:S(2)}) copy-start(s32[256]{0:T(256)} %param.23) | copy-start | bytes 3076
  13.5 0.7 %copy-start.12 = (f32[256]{0:T(256)S(1)}, f32[256]{0:T(256)}, u32[]{:S(2)}) copy-start(f32[256]{0:T(256)} %constant.25.clone.factor_z) | copy-start | bytes 3076
  14.2 0.7 %copy-start.13 = (f32[1,256]{1,0:T(1,128)S(1)}, f32[1,256]{1,0:T(1,128)}, u32[]{:S(2)}) copy-start(f32[1,256]{1,0:T(1,128)} %constant.24.clone.factor_y) | copy-start | bytes 3076
  14.8 0.7 %copy-start.14 = (f32[3]{0:T(128)S(1)}, f32[3]{0:T(128)}, u32[]{:S(2)}) copy-start(f32[3]{0:T(128)} %jet.1) | copy-start | bytes 40
  15.5 0.7 %copy-start.15 = (f32[64]{0:T(128)S(1)}, f32[64]{0:T(128)}, u32[]{:S(2)}) copy-start(f32[64]{0:T(128)} %inlet.1) | copy-start | bytes 772
where the time goes:
time: 64.5 us; the launch traced here: 63.7 us
  Pallas kernels  45.6 us (71%)
  local copies, waits for them, and re-layouts  17.5 us (27%)
  between operations  0.66 us (1%)
    pallas_call x1, Pallas kernels, local(): pl.pallas_call(kernel, out_shape=(jax.ShapeDtypeStruct(velocity.shape, f3...  45.6 us
    unnamed x36, local copies, waits for them, and re-layouts  17.5 us

commit v1 on v0

--- a/solution.py
+++ b/solution.py
@@ -105,16 +105,19 @@
 
 
 def kernel(
-    velocity, field, material, moments, nozzle, jet, inlet, rates, partners,
+    velocity_in, field_in, material_in, moments, nozzle_in, jet_in, inlet_in, rates_in, partners_in,
+    basis_z_in, inverse_z_in, forward_x_in, backward_x_in, forward_y_in, backward_y_in,
+    factor_x_in, factor_y_in, factor_z_in, masks_in,
+    new_velocity, result,
+    velocity, field, material, nozzle, jet, inlet, rates, partners,
     basis_z, inverse_z, forward_x, backward_x, forward_y, backward_y,
     factor_x, factor_y, factor_z, masks,
-    new_velocity, new_moments,
-    ext, grown, result, face_x, face_y, cut_y, coef,
-    source, send_a, recv_a, send_b, recv_b, send_c, recv_c, send_d, recv_d, poten,
-    load_sem, store_sem, halo_send, halo_recv, ssem, rsem,
+    ext, grown, face_x, face_y, cut_y, coef,
+    edge_y, source, send_a, recv_a, send_b, recv_b, send_c, recv_c, send_d, recv_d, poten,
+    load_sem, first_sem, later_sem, halo_send, halo_recv, ssem, rsem,
 ):
     wide = 16
-    classes = rates.shape[0]
+    classes = rates.shape[1]
     rows = SIDE * SIDE
     me_x = lax.axis_index("gx")
     me_grp, me_gy = lax.axis_index("grp"), lax.axis_index("gy")
@@ -127,8 +130,27 @@
     def along_y(index):
         return {"grp": index // groups, "gy": lax.rem(index, groups)}
 
+    first = [
+        pltpu.make_async_copy(src, dst, first_sem.at[number])
+        for number, (src, dst) in enumerate(
+            [(velocity_in, velocity), (field_in, field), (material_in, material), (basis_z_in, basis_z)]
+        )
+    ]
     load = pltpu.make_async_copy(moments, ext.at[pl.ds(0, classes)], load_sem)
-    load.start()
+    later = [
+        pltpu.make_async_copy(src, dst, later_sem.at[number])
+        for number, (src, dst) in enumerate(
+            [
+                (nozzle_in, nozzle), (jet_in, jet), (inlet_in, inlet), (rates_in, rates),
+                (partners_in, partners), (inverse_z_in, inverse_z), (forward_x_in, forward_x),
+                (backward_x_in, backward_x), (forward_y_in, forward_y), (backward_y_in, backward_y),
+                (factor_x_in, factor_x), (factor_y_in, factor_y), (factor_z_in, factor_z),
+                (masks_in, masks),
+            ]
+        )
+    ]
+    for copy in first + [load] + later:
+        copy.start()
     barrier = pltpu.get_barrier_semaphore()
 
     @pl.loop(1, wide)
@@ -158,6 +180,9 @@
             m[2] * f[0] - m[0] * f[2],
             m[0] * f[1] - m[1] * f[0],
         )
+
+    for copy in first:
+        copy.wait()
 
     for x in range(SIDE):
         liquid = material[x].astype(jnp.float32)
@@ -208,42 +233,52 @@
         part = pl.ds(0, (wide - 1) * wide)
         pltpu.make_async_copy(send.at[part], send.at[part], ssem.at[phase]).wait()
 
-    exchange(0, send_a, recv_a, me_y, along_y)
-
-    load.wait()
     flat = ext.reshape((classes + 3) * rows, LANES)
-    for side in range(2):
-        cut_y[side] = flat[pl.ds(side * (SIDE - 1), (classes + 3) * SIDE, stride=SIDE), :].reshape(
-            classes + 3, SIDE, LANES
-        )
     lower_x, upper_x = lax.rem(me_x + wide - 1, wide), lax.rem(me_x + 1, wide)
     lower_y, upper_y = lax.rem(me_y + wide - 1, wide), lax.rem(me_y + 1, wide)
-    halos = []
-    for number, (src, dst, device) in enumerate(
-        [
-            (cut_y.at[0], face_y.at[1], along_y(lower_y)),
-            (cut_y.at[1], face_y.at[0], along_y(upper_y)),
-            (ext.at[:, pl.ds(0, SIDE)], face_x.at[1], along_x(lower_x)),
-            (ext.at[:, pl.ds(rows - SIDE, SIDE)], face_x.at[0], along_x(upper_x)),
-        ]
-    ):
-        copy = pltpu.make_async_remote_copy(
-            src_ref=src,
-            dst_ref=dst,
-            send_sem=halo_send.at[number],
-            recv_sem=halo_recv.at[number],
-            device_id=device,
-            device_id_type=MESH,
-        )
-        copy.start()
-        halos.append(copy)
+
+    def send_faces(begin, count, number):
+        part = pl.ds(begin, count)
+        for side in range(2):
+            cut_y[side, part] = flat[
+                pl.ds(begin * rows + side * (SIDE - 1), count * SIDE, stride=SIDE), :
+            ].reshape(count, SIDE, LANES)
+        copies = []
+        for src, dst, device in (
+            (cut_y.at[0, part], face_y.at[1, part], along_y(lower_y)),
+            (cut_y.at[1, part], face_y.at[0, part], along_y(upper_y)),
+            (ext.at[part, pl.ds(0, SIDE)], face_x.at[1, part], along_x(lower_x)),
+            (ext.at[part, pl.ds(rows - SIDE, SIDE)], face_x.at[0, part], along_x(upper_x)),
+        ):
+            copy = pltpu.make_async_remote_copy(
+                src_ref=src,
+                dst_ref=dst,
+                send_sem=halo_send.at[number],
+                recv_sem=halo_recv.at[number],
+                device_id=device,
+                device_id_type=MESH,
+            )
+            copy.start()
+            copies.append(copy)
+            number += 1
+        return copies
+
+    exchange(0, send_a, recv_a, me_y, along_y)
+    moving_faces = send_faces(classes, 3, 0)
+    load.wait()
+    moment_faces = send_faces(0, classes, 4)
+    for copy in later:
+        copy.wait()
 
     square = lax.broadcasted_iota(jnp.int32, (classes, LANES), 1)
     owner = lax.broadcasted_iota(jnp.int32, (classes, LANES), 0)
-    full = jnp.zeros((classes, LANES), jnp.float32)
-    for r in range(rates.shape[1]):
-        full = full + jnp.where(partners[:, r : r + 1] == square, rates[:, r : r + 1], 0.0)
-    turned = jnp.concatenate([full, jnp.zeros((LANES - classes, LANES), jnp.float32)], 0).T[:classes]
+    label = lax.broadcasted_iota(jnp.int32, (classes, classes), 0)
+    turned = jnp.zeros((classes, classes), jnp.float32)
+    for r in range(rates.shape[0]):
+        turned = turned + jnp.where(partners[r : r + 1] == label, rates[r : r + 1], 0.0)
+    blank = jnp.zeros((classes, LANES - classes), jnp.float32)
+    turned = jnp.concatenate([turned, blank], 1)
+    full = jnp.concatenate([turned, jnp.zeros((LANES - classes, LANES), jnp.float32)], 0).T[:classes]
     low = jnp.where(square < owner, full + turned, jnp.where(square == owner, full, 0.0))
     full = full - jnp.where(owner == classes - 1, low, 0.0)
     low = jnp.where(owner > 0, roll(low, 1, 0), 0.0)
@@ -269,7 +304,7 @@
                 roll(n, 1, 0) * piece[:classes] - n * piece[classes:]
             )
 
-    pl.loop(0, rows // 2)(grow)
+    pl.loop(0, rows // 2, unroll=4)(grow)
 
     cell = lax.broadcasted_iota(jnp.int32, (rows, 1), 0)
     full_y = SIDE * wide
@@ -294,24 +329,7 @@
         )
     exchange(1, send_b, recv_b, me_x, along_x)
 
-    wave = factor_z[me_y * wide + me_x]
-    inverse = -1.0 / ((factor_x[...] + wave) + factor_y[...])
-    arrived(1, send_b, recv_b)
-    plane = dot(dot(forward_x[...], recv_b[...]), forward_y[...]) * inverse
-    send_c[...] = dot(backward_x[...], dot(plane, backward_y[...]))
-    exchange(2, send_c, recv_c, me_x, along_x)
-    arrived(2, send_c, recv_c)
-    strips = [
-        roll(recv_c[pl.ds(slot, wide, stride=SLOTS), :], -turn_of(slot), 1) for slot in range(PITCH)
-    ]
-    for by in range(wide):
-        total = jnp.zeros((wide, LANES), jnp.float32)
-        for slot in range(PITCH):
-            total = total + strips[slot] * masks[by * SLOTS + slot : by * SLOTS + slot + 1]
-        send_d[by * wide : (by + 1) * wide] = roll(total, 1 - SIDE * by, 1)
-    exchange(3, send_d, recv_d, me_y, along_y)
-
-    for copy in halos:
+    for copy in moving_faces:
         copy.wait_recv()
     has_x = [(me_x > 0).astype(jnp.float32), (me_x < wide - 1).astype(jnp.float32)]
     has_y = [(me_y > 0).astype(jnp.float32), (me_y < wide - 1).astype(jnp.float32)]
@@ -353,8 +371,10 @@
                 if x == SIDE - 1:
                     plus = plus * has_x[1]
             elif a == 1:
-                minus = jnp.where(row == 0, minus * has_y[0], minus)
-                plus = jnp.where(row == SIDE - 1, plus * has_y[1], plus)
+                edge_y[0, x : x + 1] = minus[0:1] * has_y[0]
+                edge_y[1, x : x + 1] = plus[SIDE - 1 : SIDE] * has_y[1]
+                minus = jnp.where(row == 0, 0.0, minus)
+                plus = jnp.where(row == SIDE - 1, 0.0, plus)
             else:
                 minus = jnp.where(not_first, minus, 0.0)
                 plus = jnp.where(not_last, plus, 0.0)
@@ -363,26 +383,55 @@
         coef[0, part] = 1.0 - stop - scale * total
         coef[7, part] = scale
 
+    flat_result = result.reshape(classes * rows, LANES)
+
     def advance(k):
         fill = inlet[k]
         for x in range(SIDE):
             part = slice(SIDE * x, SIDE * x + SIDE)
             here = ext[k, part]
-            below = face_x[0, k] if x == 0 else ext[k, SIDE * x - SIDE : SIDE * x]
-            above = face_x[1, k] if x == SIDE - 1 else ext[k, SIDE * x + SIDE : SIDE * x + 2 * SIDE]
-            left = jnp.where(row == 0, face_y[0, k, x : x + 1], roll(here, 1, 0))
-            right = jnp.where(row == SIDE - 1, face_y[1, k, x : x + 1], roll(here, -1, 0))
-            result[k, part] = (
+            value = (
                 (coef[0, part] * here + coef[7, part] * grown[k, part])
-                + (coef[1, part] * below + coef[2, part] * above)
-                + (coef[3, part] * left + coef[4, part] * right)
+                + (coef[3, part] * roll(here, 1, 0) + coef[4, part] * roll(here, -1, 0))
                 + (coef[5, part] * roll(here, 1, 1) + coef[6, part] * roll(here, -1, 1))
                 + coef[8, part] * fill
             )
-
-    pl.loop(0, classes)(advance)
-    store = pltpu.make_async_copy(result, new_moments, store_sem)
-    store.start()
+            if x > 0:
+                value = value + coef[1, part] * ext[k, SIDE * x - SIDE : SIDE * x]
+            if x < SIDE - 1:
+                value = value + coef[2, part] * ext[k, SIDE * x + SIDE : SIDE * x + 2 * SIDE]
+            result[k, part] = value
+
+    def finish(k):
+        for side, start in ((0, 0), (1, rows - SIDE)):
+            part = slice(start, start + SIDE)
+            result[k, part] = result[k, part] + coef[1 + side, part] * face_x[side, k]
+        for side in range(2):
+            part = pl.ds(k * rows + side * (SIDE - 1), SIDE, stride=SIDE)
+            flat_result[part, :] = flat_result[part, :] + edge_y[side] * face_y[side, k]
+
+    pl.loop(0, classes, unroll=2)(advance)
+
+    wave = factor_z[me_y * wide + me_x]
+    inverse = -1.0 / ((factor_x[...] + wave) + factor_y[...])
+    arrived(1, send_b, recv_b)
+    plane = dot(dot(forward_x[...], recv_b[...]), forward_y[...]) * inverse
+    send_c[...] = dot(backward_x[...], dot(plane, backward_y[...]))
+    exchange(2, send_c, recv_c, me_x, along_x)
+    arrived(2, send_c, recv_c)
+    strips = [
+        roll(recv_c[pl.ds(slot, wide, stride=SLOTS), :], -turn_of(slot), 1) for slot in range(PITCH)
+    ]
+    for by in range(wide):
+        total = jnp.zeros((wide, LANES), jnp.float32)
+        for slot in range(PITCH):
+            total = total + strips[slot] * masks[by * SLOTS + slot : by * SLOTS + slot + 1]
+        send_d[by * wide : (by + 1) * wide] = roll(total, 1 - SIDE * by, 1)
+    exchange(3, send_d, recv_d, me_y, along_y)
+
+    for copy in moment_faces:
+        copy.wait_recv()
+    pl.loop(0, classes, unroll=4)(finish)
 
     arrived(3, send_d, recv_d)
     poten[...] = dot(recv_d[...], inverse_z[...], ((0,), (0,)))
@@ -424,9 +473,8 @@
 
     for phase, buffer in enumerate((send_a, send_b, send_c, send_d)):
         sent(phase, buffer)
-    for copy in halos:
+    for copy in moving_faces + moment_faces:
         copy.wait_send()
-    store.wait()
 
 
 def local(velocity, moments, field, material, nozzle, jet, inlet, rates, partners):
@@ -436,48 +484,53 @@
     classes = moments.shape[0]
     rows = cells_x * cells_y
     table = tables(cells_x * width_x, cells_y * width_y, depth)
+    f32 = jnp.float32
+    operands = (
+        velocity, field, material, moments.reshape(classes, rows, depth),
+        nozzle.reshape(1, -1), jet, inlet, rates.T, partners.T,
+        table["basis_z"], table["inverse_z"], table["forward_x"], table["backward_x"],
+        table["forward_y"], table["backward_y"], table["factor_x"], table["factor_y"],
+        table["factor_z"], table["masks"],
+    )
+    scalars = (5, 6, 17)
+    here = [
+        (pltpu.SMEM if number in scalars else pltpu.VMEM)(array.shape, array.dtype)
+        for number, array in enumerate(operands)
+        if number != 3
+    ]
     vmem = pl.BlockSpec(memory_space=pltpu.VMEM)
-    smem = pl.BlockSpec(memory_space=pltpu.SMEM)
-    anywhere = pl.BlockSpec(memory_space=pl.ANY)
-    f32 = jnp.float32
+    far = pl.BlockSpec(memory_space=pltpu.HBM)
     square = pltpu.VMEM((2 * LANES, LANES), f32)
+    faces = pltpu.VMEM((2, classes + 3, SIDE, LANES), f32)
     new_velocity, new_moments = pl.pallas_call(
         kernel,
         out_shape=(
-            jax.ShapeDtypeStruct(velocity.shape, f32),
-            jax.ShapeDtypeStruct((classes, rows, depth), f32),
+            pltpu.VMEM(velocity.shape, f32),
+            pltpu.VMEM((classes, rows, depth), f32),
         ),
-        in_specs=[vmem, vmem, vmem, anywhere, vmem, smem, smem, vmem, vmem]
-        + [vmem] * 8 + [smem, vmem],
-        out_specs=(vmem, anywhere),
-        scratch_shapes=[
+        in_specs=[far] * len(operands),
+        out_specs=(vmem, vmem),
+        scratch_shapes=here + [
             pltpu.VMEM((classes + 3, rows, LANES), f32),
             pltpu.VMEM((classes, rows, LANES), f32),
-            pltpu.VMEM((classes, rows, LANES), f32),
-            pltpu.VMEM((2, classes + 3, SIDE, LANES), f32),
-            pltpu.VMEM((2, classes + 3, SIDE, LANES), f32),
-            pltpu.VMEM((2, classes + 3, SIDE, LANES), f32),
+            faces, faces, faces,
             pltpu.VMEM((9, rows, LANES), f32),
+            pltpu.VMEM((2, SIDE, LANES), f32),
             pltpu.VMEM((LANES, LANES), f32),
             square, square, square, square, square, square, square, square,
             pltpu.VMEM((LANES, LANES), f32),
             pltpu.SemaphoreType.DMA,
-            pltpu.SemaphoreType.DMA,
             pltpu.SemaphoreType.DMA((4,)),
-            pltpu.SemaphoreType.DMA((4,)),
+            pltpu.SemaphoreType.DMA((14,)),
+            pltpu.SemaphoreType.DMA((8,)),
+            pltpu.SemaphoreType.DMA((8,)),
             pltpu.SemaphoreType.DMA((4,)),
             pltpu.SemaphoreType.DMA((4,)),
         ],
         compiler_params=pltpu.CompilerParams(
-            collective_id=0, has_side_effects=True, vmem_limit_bytes=48 * 1024 * 1024
+            collective_id=0, has_side_effects=True, vmem_limit_bytes=60 * 1024 * 1024
         ),
-    )(
-        velocity, field, material, moments.reshape(classes, rows, depth),
-        nozzle.reshape(1, -1), jet, inlet, rates, partners,
-        table["basis_z"], table["inverse_z"], table["forward_x"], table["backward_x"],
-        table["forward_y"], table["backward_y"], table["factor_x"], table["factor_y"],
-        table["factor_z"], table["masks"],
-    )
+    )(*operands)
     return (new_velocity, new_moments.reshape(moments.shape))
 
 

time: 64.5 us -> 47.6 us (0.74); the launches traced: 63.7 us -> 47.5 us
  local copies, waits for them, and re-layouts: 17.5 us -> 1.96 us
  Pallas kernels: 45.6 us -> 44.9 us
    unnamed x36 -> x2, local copies, waits for them, and re-layouts: 17.5 us -> 1.96 us
    pallas_call x1, Pallas kernels: 45.6 us -> 44.9 us  [local(): pl.pallas_call(kernel, out_shape=(pltpu.VMEM(velocity.shape, f32), pltpu....]
where the time goes in v1:
time: 47.6 us; the launch traced here: 47.5 us
  Pallas kernels  44.9 us (94%)
  local copies, waits for them, and re-layouts  1.96 us (4%)
  between operations  0.64 us (1%)
    pallas_call x1, Pallas kernels, local(): pl.pallas_call(kernel, out_shape=(pltpu.VMEM(velocity.shape, f32), pltpu....  44.9 us
    unnamed x2, local copies, waits for them, and re-layouts  1.96 us

profile of v1, /device:TPU:1, one launch (start us, length us, event | category | flops | bytes accessed | tf_op | source)
XLA Modules:
  0.0 47.5 jit_solution(12140036151173394295)
XLA Ops:
  0.6 44.9 %shard_map.194 = (f32[3,8,8,128]{3,2,1,0:T(8,128)S(1)}, f32[64,64,128]{2,1,0:T(8,128)S(1)}) custom-call(f32[3,8,8,128]{3,2,1,0:T(8,128)} %velocity_in.1, f32[3,8,8,128]{3,2,1,0:T(8,128)} %field_in.1, s32[8,8,128]{2,1,0:T(8,128)} %material_in.1, f32[64,64,128]{2,1,0:T(8,128)} %bitcast.6, s32[1,256]{1,0:T(1,128)} %bitcast.9, f32[3]{0:T(128)} %jet_in.1, ...), custom_call_target="tpu_custom_call" | custom-call | tf_op jit(solution)/shard_map/pallas_call | solution.py:505
  45.6 0.6 %copy.23 = f32[3,8,8,128]{3,2,1,0:T(8,128)} copy(f32[3,8,8,128]{3,2,1,0:T(8,128)S(1)} %get-tuple-element.6) | data formatting | bytes 196608
  46.2 1.3 %copy.24 = f32[64,8,8,128]{3,2,1,0:T(8,128)} copy(f32[64,8,8,128]{3,2,1,0:T(8,128)S(1)} %bitcast.5) | data formatting | bytes 4194304

commit v2 on v1

--- a/solution.py
+++ b/solution.py
@@ -16,6 +16,8 @@
 SIDE = 8
 PITCH = 10
 SLOTS = 16
+CHAINS = 2
+STRIDE = 24
 LANES = 128
 
 
@@ -44,18 +46,20 @@
 
 def tables(full_x, full_y, depth):
     bricks_x, bricks_y = full_x // SIDE, full_y // SIDE
+    levels = bricks_x // CHAINS
     basis_x, basis_y, basis_z = real_basis(full_x), real_basis(full_y), real_basis(depth)
     inverse_x = basis_x * real_weights(full_x)[:, None]
     inverse_y = basis_y * real_weights(full_y)[:, None]
     inverse_z = basis_z * real_weights(depth)[:, None]
-    forward_x = np.zeros((2 * full_x, bricks_x * SLOTS))
-    backward_x = np.zeros((bricks_x * SLOTS, 2 * full_x))
+    forward_x = np.zeros((2 * full_x, levels * STRIDE))
+    backward_x = np.zeros((levels * STRIDE, 2 * full_x))
     for brick in range(bricks_x):
         for slot in range(PITCH):
             x = SIDE * brick + (slot if slot < SIDE else (-1 if slot == SIDE else SIDE))
             if 0 <= x < full_x:
-                forward_x[:, brick * SLOTS + slot] = basis_x[:, x]
-                backward_x[brick * SLOTS + slot] = inverse_x[:, x]
+                place = brick % levels * STRIDE + brick // levels * PITCH + slot
+                forward_x[:, place] = basis_x[:, x]
+                backward_x[place] = inverse_x[:, x]
     masks = np.zeros((bricks_y, SLOTS, LANES))
     for brick in range(bricks_y):
         for slot in range(PITCH):
@@ -123,12 +127,26 @@
     me_grp, me_gy = lax.axis_index("grp"), lax.axis_index("gy")
     groups = lax.axis_size("gy")
     me_y = me_grp * groups + me_gy
+    levels = wide // CHAINS
+    me_z = lax.rem(me_x, levels)
+    me_sheet = me_x // levels * wide + me_y
 
     def along_x(index):
         return {"gx": index}
 
     def along_y(index):
         return {"grp": index // groups, "gy": lax.rem(index, groups)}
+
+    def along_z(index):
+        return {"gx": me_x - me_z + index}
+
+    def in_sheet(index):
+        line = lax.rem(index, wide)
+        return {
+            "gx": index // wide * levels + me_z,
+            "grp": line // groups,
+            "gy": lax.rem(line, groups),
+        }
 
     first = [
         pltpu.make_async_copy(src, dst, first_sem.at[number])
@@ -153,14 +171,13 @@
         copy.start()
     barrier = pltpu.get_barrier_semaphore()
 
-    @pl.loop(1, wide)
-    def _(step):
-        pl.semaphore_signal(
-            barrier, inc=1, device_id=along_x(lax.rem(me_x + step, wide)), device_id_type=MESH
-        )
-        pl.semaphore_signal(
-            barrier, inc=1, device_id=along_y(lax.rem(me_y + step, wide)), device_id_type=MESH
-        )
+    def greet(device):
+        pl.semaphore_signal(barrier, inc=1, device_id=device, device_id_type=MESH)
+
+    pl.loop(1, CHAINS * wide)(lambda k: greet(in_sheet(lax.rem(me_sheet + k, CHAINS * wide))))
+    pl.loop(1, levels)(lambda k: greet(along_z(lax.rem(me_z + k, levels))))
+    greet(along_x(lax.rem(me_x + 1, wide)))
+    greet(along_x(lax.rem(me_x + wide - 1, wide)))
 
     lane = lax.broadcasted_iota(jnp.int32, (SIDE, LANES), 1)
     row = lax.broadcasted_iota(jnp.int32, (SIDE, LANES), 0)
@@ -206,15 +223,15 @@
     source[edge + 2 * SIDE :] = jnp.zeros((LANES - edge - 2 * SIDE, LANES), jnp.float32)
     send_a[...] = dot(basis_z[...], source[...], ((1,), (1,)))
 
-    pl.semaphore_wait(barrier, 2 * (wide - 1))
-
-    def exchange(phase, send, recv, me, target):
-        mine = pl.ds(pl.multiple_of(me * wide, wide), wide)
+    pl.semaphore_wait(barrier, CHAINS * wide + levels)
+
+    def exchange(phase, send, recv, me, target, count, size):
+        mine = pl.ds(pl.multiple_of(me * size, size), size)
 
         def start(step):
-            other = lax.rem(me + step, wide)
+            other = lax.rem(me + step, count)
             pltpu.make_async_remote_copy(
-                src_ref=send.at[pl.ds(pl.multiple_of(other * wide, wide), wide)],
+                src_ref=send.at[pl.ds(pl.multiple_of(other * size, size), size)],
                 dst_ref=recv.at[mine],
                 send_sem=ssem.at[phase],
                 recv_sem=rsem.at[phase],
@@ -222,34 +239,43 @@
                 device_id_type=MESH,
             ).start()
 
-        pl.loop(1, wide)(start)
+        pl.loop(1, count)(start)
         recv[mine] = send[mine]
 
-    def arrived(phase, send, recv):
-        part = pl.ds(0, (wide - 1) * wide)
+    def arrived(phase, recv, count, size):
+        part = pl.ds(0, (count - 1) * size)
         pltpu.make_async_copy(recv.at[part], recv.at[part], rsem.at[phase]).wait()
 
-    def sent(phase, send):
-        part = pl.ds(0, (wide - 1) * wide)
+    def sent(phase, send, count, size):
+        part = pl.ds(0, (count - 1) * size)
         pltpu.make_async_copy(send.at[part], send.at[part], ssem.at[phase]).wait()
+
+    sheet, column = (CHAINS * wide, SIDE), (levels, STRIDE)
 
     flat = ext.reshape((classes + 3) * rows, LANES)
     lower_x, upper_x = lax.rem(me_x + wide - 1, wide), lax.rem(me_x + 1, wide)
     lower_y, upper_y = lax.rem(me_y + wide - 1, wide), lax.rem(me_y + 1, wide)
 
-    def send_faces(begin, count, number):
+    moment_faces = []
+
+    def send_faces(copies, along, begin, count):
         part = pl.ds(begin, count)
-        for side in range(2):
-            cut_y[side, part] = flat[
-                pl.ds(begin * rows + side * (SIDE - 1), count * SIDE, stride=SIDE), :
-            ].reshape(count, SIDE, LANES)
-        copies = []
-        for src, dst, device in (
-            (cut_y.at[0, part], face_y.at[1, part], along_y(lower_y)),
-            (cut_y.at[1, part], face_y.at[0, part], along_y(upper_y)),
-            (ext.at[part, pl.ds(0, SIDE)], face_x.at[1, part], along_x(lower_x)),
-            (ext.at[part, pl.ds(rows - SIDE, SIDE)], face_x.at[0, part], along_x(upper_x)),
-        ):
+        if along == "y":
+            for side in range(2):
+                cut_y[side, part] = flat[
+                    pl.ds(begin * rows + side * (SIDE - 1), count * SIDE, stride=SIDE), :
+                ].reshape(count, SIDE, LANES)
+            jobs = (
+                (cut_y.at[0, part], face_y.at[1, part], along_y(lower_y)),
+                (cut_y.at[1, part], face_y.at[0, part], along_y(upper_y)),
+            )
+        else:
+            jobs = (
+                (ext.at[part, pl.ds(0, SIDE)], face_x.at[1, part], along_x(lower_x)),
+                (ext.at[part, pl.ds(rows - SIDE, SIDE)], face_x.at[0, part], along_x(upper_x)),
+            )
+        for src, dst, device in jobs:
+            number = len(moving_faces) + len(moment_faces)
             copy = pltpu.make_async_remote_copy(
                 src_ref=src,
                 dst_ref=dst,
@@ -260,13 +286,13 @@
             )
             copy.start()
             copies.append(copy)
-            number += 1
-        return copies
-
-    exchange(0, send_a, recv_a, me_y, along_y)
-    moving_faces = send_faces(classes, 3, 0)
+
+    moving_faces = []
+    exchange(0, send_a, recv_a, me_sheet, in_sheet, *sheet)
+    send_faces(moving_faces, "y", classes, 3)
+    send_faces(moving_faces, "x", classes, 3)
     load.wait()
-    moment_faces = send_faces(0, classes, 4)
+    send_faces(moment_faces, "x", 0, 32)
     for copy in later:
         copy.wait()
 
@@ -285,8 +311,8 @@
     both = jnp.concatenate([low, full], 0)
     high_part = both.astype(jnp.bfloat16).astype(jnp.float32)
     low_part = both - high_part
-    column = lax.broadcasted_iota(jnp.int32, (2 * classes, LANES), 1)
-    weights = jnp.where(column < classes, high_part, roll(low_part, classes, 1)).astype(jnp.bfloat16)
+    place = lax.broadcasted_iota(jnp.int32, (2 * classes, LANES), 1)
+    weights = jnp.where(place < classes, high_part, roll(low_part, classes, 1)).astype(jnp.bfloat16)
     flat_grown = grown.reshape(classes * rows, LANES)
 
     def grow(pair):
@@ -315,19 +341,22 @@
     deep = lax.broadcasted_iota(jnp.int32, (rows, LANES), 1)
     coef[8] = jnp.where(deep == 0, hit[0], jnp.where(deep == 1, hit[1], 0.0))
 
-    arrived(0, send_a, recv_a)
-    strips = [jnp.zeros((wide, LANES), jnp.float32) for _ in range(PITCH)]
-    for by in range(wide):
-        line = roll(recv_a[by * wide : (by + 1) * wide], SIDE * by - 1, 1)
+    arrived(0, recv_a, *sheet)
+    for chain in range(CHAINS):
+        strips = [jnp.zeros((levels, LANES), jnp.float32) for _ in range(PITCH)]
+        for by in range(wide):
+            place = (chain * wide + by) * SIDE
+            line = roll(recv_a[place : place + SIDE], SIDE * by - 1, 1)
+            for slot in range(PITCH):
+                strips[slot] = strips[slot] + line * masks[by * SLOTS + slot : by * SLOTS + slot + 1]
         for slot in range(PITCH):
-            strips[slot] = strips[slot] + line * masks[by * SLOTS + slot : by * SLOTS + slot + 1]
-    for slot in range(SLOTS):
-        send_b[pl.ds(slot, wide, stride=SLOTS), :] = (
-            roll(strips[slot], turn_of(slot), 1)
-            if slot < PITCH
-            else jnp.zeros((wide, LANES), jnp.float32)
-        )
-    exchange(1, send_b, recv_b, me_x, along_x)
+            send_b[pl.ds(chain * PITCH + slot, levels, stride=STRIDE), :] = roll(
+                strips[slot], turn_of(slot), 1
+            )
+    for slot in range(CHAINS * PITCH, STRIDE):
+        send_b[pl.ds(slot, levels, stride=STRIDE), :] = jnp.zeros((levels, LANES), jnp.float32)
+    exchange(1, send_b, recv_b, me_z, along_z, *column)
+    send_faces(moment_faces, "y", 0, 32)
 
     for copy in moving_faces:
         copy.wait_recv()
@@ -412,28 +441,33 @@
 
     pl.loop(0, classes, unroll=2)(advance)
 
-    wave = factor_z[me_y * wide + me_x]
+    wave = factor_z[me_sheet * levels + me_z]
     inverse = -1.0 / ((factor_x[...] + wave) + factor_y[...])
-    arrived(1, send_b, recv_b)
+    arrived(1, recv_b, *column)
     plane = dot(dot(forward_x[...], recv_b[...]), forward_y[...]) * inverse
     send_c[...] = dot(backward_x[...], dot(plane, backward_y[...]))
-    exchange(2, send_c, recv_c, me_x, along_x)
-    arrived(2, send_c, recv_c)
-    strips = [
-        roll(recv_c[pl.ds(slot, wide, stride=SLOTS), :], -turn_of(slot), 1) for slot in range(PITCH)
-    ]
-    for by in range(wide):
-        total = jnp.zeros((wide, LANES), jnp.float32)
-        for slot in range(PITCH):
-            total = total + strips[slot] * masks[by * SLOTS + slot : by * SLOTS + slot + 1]
-        send_d[by * wide : (by + 1) * wide] = roll(total, 1 - SIDE * by, 1)
-    exchange(3, send_d, recv_d, me_y, along_y)
+    exchange(2, send_c, recv_c, me_z, along_z, *column)
+    send_faces(moment_faces, "y", 32, 32)
+    arrived(2, recv_c, *column)
+    for chain in range(CHAINS):
+        strips = [
+            roll(recv_c[pl.ds(chain * PITCH + slot, levels, stride=STRIDE), :], -turn_of(slot), 1)
+            for slot in range(PITCH)
+        ]
+        for by in range(wide):
+            total = jnp.zeros((levels, LANES), jnp.float32)
+            for slot in range(PITCH):
+                total = total + strips[slot] * masks[by * SLOTS + slot : by * SLOTS + slot + 1]
+            place = (chain * wide + by) * SIDE
+            send_d[place : place + SIDE] = roll(total, 1 - SIDE * by, 1)
+    exchange(3, send_d, recv_d, me_sheet, in_sheet, *sheet)
+    send_faces(moment_faces, "x", 32, 32)
 
     for copy in moment_faces:
         copy.wait_recv()
     pl.loop(0, classes, unroll=4)(finish)
 
-    arrived(3, send_d, recv_d)
+    arrived(3, recv_d, *sheet)
     poten[...] = dot(recv_d[...], inverse_z[...], ((0,), (0,)))
     for x in range(SIDE):
         part = slice(SIDE * x, SIDE * x + SIDE)
@@ -471,8 +505,10 @@
             value = liquid * (here + step_size * (lorentz[a] + viscosity * spread))
             new_velocity[a, x] = jnp.where(stop, jet[a], value)
 
-    for phase, buffer in enumerate((send_a, send_b, send_c, send_d)):
-        sent(phase, buffer)
+    for phase, buffer, shape in (
+        (0, send_a, sheet), (1, send_b, column), (2, send_c, column), (3, send_d, sheet),
+    ):
+        sent(phase, buffer, *shape)
     for copy in moving_faces + moment_faces:
         copy.wait_send()
 
@@ -501,6 +537,7 @@
     vmem = pl.BlockSpec(memory_space=pltpu.VMEM)
     far = pl.BlockSpec(memory_space=pltpu.HBM)
     square = pltpu.VMEM((2 * LANES, LANES), f32)
+    narrow = pltpu.VMEM((width_x // CHAINS * STRIDE, LANES), f32)
     faces = pltpu.VMEM((2, classes + 3, SIDE, LANES), f32)
     new_velocity, new_moments = pl.pallas_call(
         kernel,
@@ -517,13 +554,13 @@
             pltpu.VMEM((9, rows, LANES), f32),
             pltpu.VMEM((2, SIDE, LANES), f32),
             pltpu.VMEM((LANES, LANES), f32),
-            square, square, square, square, square, square, square, square,
+            square, square, narrow, narrow, narrow, narrow, square, square,
             pltpu.VMEM((LANES, LANES), f32),
             pltpu.SemaphoreType.DMA,
             pltpu.SemaphoreType.DMA((4,)),
             pltpu.SemaphoreType.DMA((14,)),
-            pltpu.SemaphoreType.DMA((8,)),
-            pltpu.SemaphoreType.DMA((8,)),
+            pltpu.SemaphoreType.DMA((16,)),
+            pltpu.SemaphoreType.DMA((16,)),
             pltpu.SemaphoreType.DMA((4,)),
             pltpu.SemaphoreType.DMA((4,)),
         ],

time: 47.6 us -> 41.2 us (0.87)
  Pallas kernels: 44.9 us -> 38.4 us
    pallas_call x1, Pallas kernels: 44.9 us -> 38.4 us  [local(): pl.pallas_call(kernel, out_shape=(pltpu.VMEM(velocity.shape, f32), pltpu....]
where the time goes in v2:
time: 41.2 us; the launch traced here: 41 us
  Pallas kernels  38.4 us (93%)
  local copies, waits for them, and re-layouts  1.96 us (5%)
  between operations  0.64 us (2%)
    pallas_call x1, Pallas kernels, local(): pl.pallas_call(kernel, out_shape=(pltpu.VMEM(velocity.shape, f32), pltpu....  38.4 us
    unnamed x2, local copies, waits for them, and re-layouts  1.96 us

profile of v2, /device:TPU:1, one launch (start us, length us, event | category | flops | bytes accessed | tf_op | source)
XLA Modules:
  0.0 41.0 jit_solution(10053982059725709995)
XLA Ops:
  0.6 38.4 %shard_map.194 = (f32[3,8,8,128]{3,2,1,0:T(8,128)S(1)}, f32[64,64,128]{2,1,0:T(8,128)S(1)}) custom-call(f32[3,8,8,128]{3,2,1,0:T(8,128)} %velocity_in.1, f32[3,8,8,128]{3,2,1,0:T(8,128)} %field_in.1, s32[8,8,128]{2,1,0:T(8,128)} %material_in.1, f32[64,64,128]{2,1,0:T(8,128)} %bitcast.6, s32[1,256]{1,0:T(1,128)} %bitcast.9, f32[3]{0:T(128)} %jet_in.1, ...), custom_call_target="tpu_custom_call" | custom-call | tf_op jit(solution)/shard_map/pallas_call | solution.py:542
  39.0 0.6 %copy.23 = f32[3,8,8,128]{3,2,1,0:T(8,128)} copy(f32[3,8,8,128]{3,2,1,0:T(8,128)S(1)} %get-tuple-element.6) | data formatting | bytes 196608
  39.7 1.3 %copy.24 = f32[64,8,8,128]{3,2,1,0:T(8,128)} copy(f32[64,8,8,128]{3,2,1,0:T(8,128)S(1)} %bitcast.5) | data formatting | bytes 4194304

commit v3 on v2

--- a/solution.py
+++ b/solution.py
@@ -103,7 +103,7 @@
         first,
         second,
         (dims, ((), ())),
-        precision=lax.Precision.HIGHEST,
+        precision=lax.Precision.HIGH,
         preferred_element_type=jnp.float32,
     )
 
@@ -431,10 +431,12 @@
                 value = value + coef[2, part] * ext[k, SIDE * x + SIDE : SIDE * x + 2 * SIDE]
             result[k, part] = value
 
-    def finish(k):
+    def finish_x(k):
         for side, start in ((0, 0), (1, rows - SIDE)):
             part = slice(start, start + SIDE)
             result[k, part] = result[k, part] + coef[1 + side, part] * face_x[side, k]
+
+    def finish_y(k):
         for side in range(2):
             part = pl.ds(k * rows + side * (SIDE - 1), SIDE, stride=SIDE)
             flat_result[part, :] = flat_result[part, :] + edge_y[side] * face_y[side, k]
@@ -448,6 +450,25 @@
     send_c[...] = dot(backward_x[...], dot(plane, backward_y[...]))
     exchange(2, send_c, recv_c, me_z, along_z, *column)
     send_faces(moment_faces, "y", 32, 32)
+    for x in range(SIDE):
+        part = slice(SIDE * x, SIDE * x + SIDE)
+        c = current_at(x)
+        f = [field[a, x] for a in range(3)]
+        lorentz = (c[1] * f[2] - c[2] * f[1], c[2] * f[0] - c[0] * f[2], c[0] * f[1] - c[1] * f[0])
+        liquid = material[x].astype(jnp.float32)
+        stop = coef[8, part] > 0.5
+        for a in range(3):
+            here = moving_at(a, x)
+            below, above = around_y(a, x)
+            spread = (
+                (moving_at(a, x - 1) + moving_at(a, x + 1))
+                + (below + above)
+                + (down_z(here) + up_z(here))
+                - 6.0 * here
+            )
+            value = liquid * (here + step_size * (lorentz[a] + viscosity * spread))
+            new_velocity[a, x] = jnp.where(stop, jet[a], value)
+
     arrived(2, recv_c, *column)
     for chain in range(CHAINS):
         strips = [
@@ -463,9 +484,13 @@
     exchange(3, send_d, recv_d, me_sheet, in_sheet, *sheet)
     send_faces(moment_faces, "x", 32, 32)
 
-    for copy in moment_faces:
+    for copy in moment_faces[:4]:
         copy.wait_recv()
-    pl.loop(0, classes, unroll=4)(finish)
+    pl.loop(0, classes // 2, unroll=4)(finish_x)
+    pl.loop(0, classes // 2, unroll=4)(finish_y)
+    for copy in moment_faces[4:6]:
+        copy.wait_recv()
+    pl.loop(classes // 2, classes, unroll=4)(finish_y)
 
     arrived(3, recv_d, *sheet)
     poten[...] = dot(recv_d[...], inverse_z[...], ((0,), (0,)))
@@ -487,23 +512,18 @@
             0.5 * (high_y - low_y),
             0.5 * (up_z(middle) - down_z(middle)),
         )
-        c = current_at(x)
-        d = [c[a] - gradient[a] for a in range(3)]
         f = [field[a, x] for a in range(3)]
-        lorentz = (d[1] * f[2] - d[2] * f[1], d[2] * f[0] - d[0] * f[2], d[0] * f[1] - d[1] * f[0])
-        liquid = material[x].astype(jnp.float32)
-        stop = coef[8, part] > 0.5
+        pull = (
+            gradient[1] * f[2] - gradient[2] * f[1],
+            gradient[2] * f[0] - gradient[0] * f[2],
+            gradient[0] * f[1] - gradient[1] * f[0],
+        )
         for a in range(3):
-            here = moving_at(a, x)
-            below, above = around_y(a, x)
-            spread = (
-                (moving_at(a, x - 1) + moving_at(a, x + 1))
-                + (below + above)
-                + (down_z(here) + up_z(here))
-                - 6.0 * here
-            )
-            value = liquid * (here + step_size * (lorentz[a] + viscosity * spread))
-            new_velocity[a, x] = jnp.where(stop, jet[a], value)
+            new_velocity[a, x] = new_velocity[a, x] - coef[7, part] * pull[a]
+
+    for copy in moment_faces[6:]:
+        copy.wait_recv()
+    pl.loop(classes // 2, classes, unroll=4)(finish_x)
 
     for phase, buffer, shape in (
         (0, send_a, sheet), (1, send_b, column), (2, send_c, column), (3, send_d, sheet),

time: 41.2 us -> 40.4 us (0.981)
  Pallas kernels: 38.4 us -> 37.6 us
    pallas_call x1, Pallas kernels: 38.4 us -> 37.6 us  [local(): pl.pallas_call(kernel, out_shape=(pltpu.VMEM(velocity.shape, f32), pltpu....]
where the time goes in v3:
time: 40.4 us; the launch traced here: 40.2 us
  Pallas kernels  37.6 us (93%)
  local copies, waits for them, and re-layouts  1.96 us (5%)
  between operations  0.64 us (2%)
    pallas_call x1, Pallas kernels, local(): pl.pallas_call(kernel, out_shape=(pltpu.VMEM(velocity.shape, f32), pltpu....  37.6 us
    unnamed x2, local copies, waits for them, and re-layouts  1.96 us

profile of v3, /device:TPU:1, one launch (start us, length us, event | category | flops | bytes accessed | tf_op | source)
XLA Modules:
  0.0 40.2 jit_solution(18270030203573429263)
XLA Ops:
  0.6 37.6 %shard_map.194 = (f32[3,8,8,128]{3,2,1,0:T(8,128)S(1)}, f32[64,64,128]{2,1,0:T(8,128)S(1)}) custom-call(f32[3,8,8,128]{3,2,1,0:T(8,128)} %velocity_in.1, f32[3,8,8,128]{3,2,1,0:T(8,128)} %field_in.1, s32[8,8,128]{2,1,0:T(8,128)} %material_in.1, f32[64,64,128]{2,1,0:T(8,128)} %bitcast.6, s32[1,256]{1,0:T(1,128)} %bitcast.9, f32[3]{0:T(128)} %jet_in.1, ...), custom_call_target="tpu_custom_call" | custom-call | tf_op jit(solution)/shard_map/pallas_call | solution.py:562
  38.2 0.6 %copy.23 = f32[3,8,8,128]{3,2,1,0:T(8,128)} copy(f32[3,8,8,128]{3,2,1,0:T(8,128)S(1)} %get-tuple-element.6) | data formatting | bytes 196608
  38.9 1.3 %copy.24 = f32[64,8,8,128]{3,2,1,0:T(8,128)} copy(f32[64,8,8,128]{3,2,1,0:T(8,128)S(1)} %bitcast.5) | data formatting | bytes 4194304

commit v4 on v3

--- a/solution.py
+++ b/solution.py
@@ -292,7 +292,6 @@
     send_faces(moving_faces, "y", classes, 3)
     send_faces(moving_faces, "x", classes, 3)
     load.wait()
-    send_faces(moment_faces, "x", 0, 32)
     for copy in later:
         copy.wait()
 
@@ -330,7 +329,9 @@
                 roll(n, 1, 0) * piece[:classes] - n * piece[classes:]
             )
 
-    pl.loop(0, rows // 2, unroll=4)(grow)
+    pl.loop(0, rows // 4, unroll=4)(grow)
+    send_faces(moment_faces, "x", 0, 32)
+    pl.loop(rows // 4, rows // 2, unroll=4)(grow)
 
     cell = lax.broadcasted_iota(jnp.int32, (rows, 1), 0)
     full_y = SIDE * wide

time: 40.4 us -> 38.6 us (0.955)
  Pallas kernels: 37.6 us -> 35.9 us
    pallas_call x1, Pallas kernels: 37.6 us -> 35.9 us  [local(): pl.pallas_call(kernel, out_shape=(pltpu.VMEM(velocity.shape, f32), pltpu....]
where the time goes in v4:
time: 38.6 us; the launch traced here: 38.5 us
  Pallas kernels  35.9 us (93%)
  local copies, waits for them, and re-layouts  1.96 us (5%)
  between operations  0.64 us (2%)
    pallas_call x1, Pallas kernels, local(): pl.pallas_call(kernel, out_shape=(pltpu.VMEM(velocity.shape, f32), pltpu....  35.9 us
    unnamed x2, local copies, waits for them, and re-layouts  1.96 us

profile of v4, /device:TPU:1, one launch (start us, length us, event | category | flops | bytes accessed | tf_op | source)
XLA Modules:
  0.0 38.5 jit_solution(1336899483026092380)
XLA Ops:
  0.6 35.9 %shard_map.194 = (f32[3,8,8,128]{3,2,1,0:T(8,128)S(1)}, f32[64,64,128]{2,1,0:T(8,128)S(1)}) custom-call(f32[3,8,8,128]{3,2,1,0:T(8,128)} %velocity_in.1, f32[3,8,8,128]{3,2,1,0:T(8,128)} %field_in.1, s32[8,8,128]{2,1,0:T(8,128)} %material_in.1, f32[64,64,128]{2,1,0:T(8,128)} %bitcast.6, s32[1,256]{1,0:T(1,128)} %bitcast.9, f32[3]{0:T(128)} %jet_in.1, ...), custom_call_target="tpu_custom_call" | custom-call | tf_op jit(solution)/shard_map/pallas_call | solution.py:563
  36.5 0.6 %copy.23 = f32[3,8,8,128]{3,2,1,0:T(8,128)} copy(f32[3,8,8,128]{3,2,1,0:T(8,128)S(1)} %get-tuple-element.6) | data formatting | bytes 196608
  37.2 1.3 %copy.24 = f32[64,8,8,128]{3,2,1,0:T(8,128)} copy(f32[64,8,8,128]{3,2,1,0:T(8,128)S(1)} %bitcast.5) | data formatting | bytes 4194304

commit v5 on v4

--- a/solution.py
+++ b/solution.py
@@ -329,9 +329,9 @@
                 roll(n, 1, 0) * piece[:classes] - n * piece[classes:]
             )
 
-    pl.loop(0, rows // 4, unroll=4)(grow)
+    pl.loop(0, rows * 3 // 16, unroll=4)(grow)
     send_faces(moment_faces, "x", 0, 32)
-    pl.loop(rows // 4, rows // 2, unroll=4)(grow)
+    pl.loop(rows * 3 // 16, rows // 2, unroll=4)(grow)
 
     cell = lax.broadcasted_iota(jnp.int32, (rows, 1), 0)
     full_y = SIDE * wide

time: 38.6 us -> 38.8 us (level)
  no operation moved by 1% of the time
where the time goes in v5:
time: 38.8 us; the launch traced here: 38.7 us
  Pallas kernels  36.1 us (93%)
  local copies, waits for them, and re-layouts  1.96 us (5%)
  between operations  0.64 us (2%)
    pallas_call x1, Pallas kernels, local(): pl.pallas_call(kernel, out_shape=(pltpu.VMEM(velocity.shape, f32), pltpu....  36.1 us
    unnamed x2, local copies, waits for them, and re-layouts  1.96 us

profile of v5, /device:TPU:1, one launch (start us, length us, event | category | flops | bytes accessed | tf_op | source)
XLA Modules:
  0.0 38.7 jit_solution(13756719872714050342)
XLA Ops:
  0.6 36.1 %shard_map.194 = (f32[3,8,8,128]{3,2,1,0:T(8,128)S(1)}, f32[64,64,128]{2,1,0:T(8,128)S(1)}) custom-call(f32[3,8,8,128]{3,2,1,0:T(8,128)} %velocity_in.1, f32[3,8,8,128]{3,2,1,0:T(8,128)} %field_in.1, s32[8,8,128]{2,1,0:T(8,128)} %material_in.1, f32[64,64,128]{2,1,0:T(8,128)} %bitcast.6, s32[1,256]{1,0:T(1,128)} %bitcast.9, f32[3]{0:T(128)} %jet_in.1, ...), custom_call_target="tpu_custom_call" | custom-call | tf_op jit(solution)/shard_map/pallas_call | solution.py:563
  36.8 0.6 %copy.23 = f32[3,8,8,128]{3,2,1,0:T(8,128)} copy(f32[3,8,8,128]{3,2,1,0:T(8,128)S(1)} %get-tuple-element.6) | data formatting | bytes 196608
  37.4 1.3 %copy.24 = f32[64,8,8,128]{3,2,1,0:T(8,128)} copy(f32[64,8,8,128]{3,2,1,0:T(8,128)S(1)} %bitcast.5) | data formatting | bytes 4194304
